TPU v7x, 1024 devices: a whole 4x4x32 slice. The times are simulated.
1024 devices in a mesh: row: 32 (over z_lo, y), col: 32 (over z_hi, x, core).
Axes of the slice: x: 4, y: 4, z: 32 (z_hi: 4, z_lo: 8; z = z_hi * 8 + z_lo), core: 2. Of those that a mesh axis runs over, the one named last changes fastest.
Arguments:
- factor_panel: bfloat16 [32768, 1024], P('row', 'col'), may hold values from -0.03125 to 0.03125
- ancestor_inverse: bfloat16 [32768, 32768], P('row', 'col'), may hold values from -6 to 6
- pattern: int32 [256], replicated, may hold values 0 or 1
- diag_base: float32 [1024], P('col'), may hold values from 0.5 to 2
Outputs:
- offdiag_inverse: bfloat16 [32768, 1024], P('row', 'col')
- diag_inverse: float32 [1024], P('col')
All inputs are finite; a program needn't handle non-finite values.
Results may differ from a plain program's by a relative error of at most 0.0044.
Values may be sent and summed in bfloat16 or wider, within the bound.
A program may use at most 32 MiB of HBM per device.

v0:
```python
import jax
import jax.numpy as jnp
from jax import lax
from jax.sharding import PartitionSpec as P

BLOCK = 128


def spread(array, axis, root):
    mine = lax.axis_index(axis) == root
    return lax.psum(jnp.where(mine, array, jnp.zeros_like(array)), axis)


def body(factor_panel, ancestor_inverse, pattern, diag_base):
    rows_dev = ancestor_inverse.shape[0]
    row_index = lax.axis_index("row")
    col_index = lax.axis_index("col")
    blocks_per = lax.axis_size("row") // lax.axis_size("col")
    full_mask = jnp.repeat(pattern.astype(jnp.float32), BLOCK)
    own_mask = lax.dynamic_slice_in_dim(full_mask, row_index * rows_dev, rows_dev, 0)
    masked_own = factor_panel * own_mask[:, None].astype(jnp.bfloat16)
    panel = lax.all_gather(masked_own, "col", axis=1, tiled=True)
    crossed = spread(panel, "row", col_index * blocks_per + 0)
    product = jnp.dot(ancestor_inverse, crossed, preferred_element_type=jnp.float32)
    summed = lax.psum_scatter(product, "col", scatter_dimension=1, tiled=True)
    offdiag_inverse = (-(own_mask[:, None] * summed)).astype(jnp.bfloat16)
    local_diag = jnp.sum(masked_own.astype(jnp.float32) * summed, axis=0)
    diag_inverse = diag_base + lax.psum(local_diag, "row")
    return (offdiag_inverse, diag_inverse)


def solution(mesh):
    placed = (P("row", "col"), P("row", "col"), P(), P("col"))
    return jax.shard_map(
        body, mesh=mesh, in_specs=placed, out_specs=(P("row", "col"), P("col")), check_vma=False
    )
```

profile of v0, /device:TPU:4, one launch (start us, length us, event | category | flops | bytes accessed | tf_op | source)
XLA Modules:
  0.0 987.0 jit_solution(11720073511502217731)
XLA Ops:
  7.2 0.0 copy-start
  7.2 0.0 all-gather.2.cloned.1.call-start
  7.2 0.8 convert_element_type.13
  8.1 0.1 broadcast_bitcast_fusion
  8.2 1.5 broadcast_multiply_fusion
  9.6 0.0 all-gather.2.cloned.1.call-update
  9.7 0.0 all-reduce.2.cloned.1.call-start
  9.7 141.0 %all-gather.2.cloned.1.call-done = bf16[1024,1024]{0,1:T(8,128)(2,1)} async-done(((bf16[1024,32]{0,1:T(8,128)(2,1)}), bf16[1024,1024]{0,1:T(8,128)(2,1)}) %all-gather.2.cloned.1.call-update) | async-done | bytes 2097168 | tf_op jit(solution)/shard_map/all_gather | solution.py:22
  150.7 1.5 broadcast_select_fusion
  152.2 0.0 all-reduce.2.cloned.1.call-update
  152.2 0.0 reduce-scatter.2.cloned.1.call-start
  152.3 471.5 %all-reduce.2.cloned.1.call-done = bf16[1024,1024]{0,1:T(8,128)(2,1)} async-done(((bf16[1024,1024]{0,1:T(8,128)(2,1)}), bf16[1024,1024]{0,1:T(8,128)(2,1)}) %all-reduce.2.cloned.1.call-update) | async-done | bytes 2097168 | tf_op jit(solution)/shard_map/psum | solution.py:11
  623.8 0.0 copy-done
  623.8 5.9 convolution_bitcast_fusion
  629.7 0.0 copy-start.1
  629.7 0.0 copy-start.2
  629.7 0.0 reduce-scatter.2.cloned.1.call-update
  629.8 226.3 %reduce-scatter.2.cloned.1.call-done = f32[1024,32]{0,1:T(8,128)} async-done(((f32[1024,1024]{0,1:T(8,128)}), f32[1024,32]{0,1:T(8,128)}) %reduce-scatter.2.cloned.1.call-update) | async-done | bytes 131088 | tf_op jit(solution)/shard_map/reduce_scatter | solution.py:25
  856.1 0.0 copy-done.1
  856.1 1.7 multiply_reduce_fusion
  857.7 122.3 %psum.15 = f32[32]{0:T(128)S(1)} all-reduce(f32[32]{0:T(128)S(1)} %get-tuple-element.4), channel_id=1, replica_groups=mesh['row'=32,'col'=32] {'row'}, use_global_device_ids=true, to_apply=%region_3.4 | all-reduce | flops 32 | bytes 256 | tf_op jit(solution)/shard_map/psum | solution.py:28
  980.0 0.0 copy-done.2
  980.0 0.5 add.13
  (1 shorter events, 0.0 us)
Async XLA Ops:
  7.2 616.7 %copy-start = (bf16[1024,1024]{1,0:T(8,128)(2,1)S(1)}, bf16[1024,1024]{1,0:T(8,128)(2,1)}, u32[]{:S(2)}) copy-start(bf16[1024,1024]{1,0:T(8,128)(2,1)} %param.5) | copy-start | bytes 6291460
  7.2 143.6 %all-gather.2.cloned.1.call-start = ((), (), s32[]{:S(2)}) async-start(), calls=%async_computation.1 | async-start | bytes 2162688 | tf_op jit(solution)/shard_map/all_gather | solution.py:22
  9.7 614.2 %all-reduce.2.cloned.1.call-start = ((), (), s32[]{:S(2)}) async-start(), calls=%async_computation.2 | async-start | bytes 4194304 | tf_op jit(solution)/shard_map/psum | solution.py:11
  152.2 703.8 %reduce-scatter.2.cloned.1.call-start = ((), (), s32[]{:S(2)}) async-start(), calls=%async_computation.3 | async-start | bytes 4325376 | tf_op jit(solution)/shard_map/reduce_scatter | solution.py:25
  629.7 226.3 %copy-start.1 = (bf16[1024,32]{0,1:T(8,128)(2,1)S(1)}, bf16[1024,32]{0,1:T(8,128)(2,1)}, u32[]{:S(2)}) copy-start(bf16[1024,32]{0,1:T(8,128)(2,1)} %param.4) | copy-start | bytes 196612
  629.7 350.3 %copy-start.2 = (f32[32]{0:T(128)S(1)}, f32[32]{0:T(128)}, u32[]{:S(2)}) copy-start(f32[32]{0:T(128)} %param.7) | copy-start | bytes 388
Sparse Core Ops, SparseCore 0:
  12.9 137.8 all-gather.1
  154.2 469.5 all-reduce.1
  630.5 225.5 reduce-scatter.1
where the time goes:
time: 987 us
  waiting for transfers between devices  839 us (85%)
  blocking collectives  122 us (12%)
  between operations  13.8 us (1%)
    psum x1, waiting for transfers between devices, spread(): return lax.psum(jnp.where(mine, array, jnp.zeros_like(array)), axis)  472 us
    reduce_scatter x1, waiting for transfers between devices, body(): summed = lax.psum_scatter(product, 'col', scatter_dimension=1, tiled=True)  226 us
    all_gather x1, waiting for transfers between devices, body(): panel = lax.all_gather(masked_own, 'col', axis=1, tiled=True)  141 us
    psum x1, blocking collectives, body(): diag_inverse = diag_base + lax.psum(local_diag, 'row')  122 us
  transfers between devices with their start and end apart: 3, of which 3 were waited for; matrix products, arithmetic and copies ran while one was open for 0% of the time, Pallas kernels for 0%

commit v1 on v0

v1 whole, which is shorter than its diff:
```python
import functools

import jax
import jax.numpy as jnp
from jax import lax
from jax.experimental import pallas as pl
from jax.experimental.pallas import tpu as pltpu
from jax.sharding import PartitionSpec as P

MESH = pl.DeviceIdType.MESH
BF16 = jnp.bfloat16
F32 = jnp.float32
OFFS = (1, 3, 2, 0)


def aligned(i, n):
    return pl.multiple_of(i * n, n)


def kernel(pattern_ref, f_ref, base_ref, a_hbm, out_ref, diag_ref,
           a_ref, mask_ref, ft_ref, g_ref, p_ref, cs_ref, cr_ref, xs_ref, xr_ref, xo_ref,
           zs_ref, zr_ref, dz_ref, dy_ref,
           a_sem, ts, tr, zs, zr, ys, yr, cs, cr, xs, xr, hs, hr, ds_, dr, es, er):
    r, c = lax.axis_index("row"), lax.axis_index("col")
    zl, y = r // 4, r % 4
    zh, x, k = c // 8, (c // 2) % 4, c % 2
    half, q = zl // 4, zl % 4

    def row_of(zl_, y_):
        return zl_ * 4 + y_

    def col_of(zh_, x_, k_):
        return (zh_ * 4 + x_) * 2 + k_

    barrier = pltpu.get_barrier_semaphore()

    def greet(dev):
        pl.semaphore_signal(barrier, inc=1, device_id=dev, device_id_type=MESH)

    a_copy = pltpu.make_async_copy(a_hbm, a_ref, a_sem)
    a_copy.start()
    for i in range(8):
        src_col = (i // 2 * 4 + y) * 2 + i % 2
        pl.when(jnp.logical_or(c != r, src_col != c))(lambda s=src_col: greet((c, s)))
    for o in range(1, 8):
        greet((row_of((zl + o) % 8, y), c))
    for o in range(1, 4):
        greet((row_of(zl, (y + o) % 4), c))
        greet((r, col_of(zh, (x + o) % 4, k)))
        greet((r, col_of((zh + o) % 4, x, k)))
    greet((r, col_of(zh, x, 1 - k)))

    for b in range(8):
        m = pattern_ref[r * 8 + b].astype(F32)
        mask_ref[:, b * 128:(b + 1) * 128] = jnp.full((32, 128), m, F32)
    ft_ref[...] = (f_ref[...].astype(F32) * mask_ref[...]).astype(BF16)

    self_t = jnp.logical_and(c == r, row_of(zl, x) == r)
    pl.semaphore_wait(barrier, 25 - self_t.astype(jnp.int32))

    pending = []
    t_rows = pl.ds(aligned(c, 32), 32)
    t_copies = []
    for h in range(2):
        for p in range(4):
            lanes = pl.ds(p * 256, 256)
            there = row_of(h * 4 + p, x)
            here = jnp.logical_and(c == r, there == r)
            remote = pltpu.make_async_remote_copy(
                ft_ref.at[:, lanes], g_ref.at[t_rows, lanes], ts.at[h * 4 + p], tr.at[zh * 2 + k],
                device_id=(there, r), device_id_type=MESH)
            local = pltpu.make_async_copy(
                ft_ref.at[:, lanes], g_ref.at[t_rows, lanes], tr.at[zh * 2 + k])
            pl.when(jnp.logical_not(here))(remote.start)
            pl.when(here)(local.start)
            t_copies.append((here, remote))

    def w_of(j):
        return (zh + OFFS[j]) % 4

    q_lanes = pl.ds(aligned(q, 256), 256)

    def z_copies(j):
        rows = pl.ds(aligned(w_of(j) * 4 + y, 64), 64)
        return [pltpu.make_async_remote_copy(
            g_ref.at[rows, q_lanes], g_ref.at[rows, q_lanes], zs.at[j * 3 + o - 1], zr.at[w_of(j) * 3 + o - 1],
            device_id=(row_of(half * 4 + (q + o) % 4, y), c), device_id_type=MESH) for o in range(1, 4)]

    def y_copies(j):
        rows = pl.ds(aligned(w_of(j) * 4 + y, 64), 64)
        return [pltpu.make_async_remote_copy(
            g_ref.at[rows, :], g_ref.at[rows, :], ys.at[j * 3 + o - 1], yr.at[w_of(j) * 3 + o - 1],
            device_id=(row_of(zl, (y + o) % 4), c), device_id_type=MESH) for o in range(1, 4)]

    def core_copy(j):
        return pltpu.make_async_remote_copy(
            cs_ref.at[j], cr_ref.at[j], cs.at[j], cr.at[j],
            device_id=(r, col_of(zh, x, 1 - k)), device_id_type=MESH)

    def x_copies(j):
        return [pltpu.make_async_remote_copy(
            xs_ref.at[j, o - 1], xr_ref.at[j, o - 1], xs.at[j * 3 + o - 1], xr.at[j * 3 + o - 1],
            device_id=(r, col_of(zh, (x + o) % 4, k)), device_id_type=MESH) for o in range(1, 4)]

    def h_copy(o):
        return pltpu.make_async_remote_copy(
            zs_ref.at[o - 1], zr_ref.at[o - 1], hs.at[o - 1], hr.at[o - 1],
            device_id=(r, col_of((zh + o) % 4, x, k)), device_id_type=MESH)

    def send(copies):
        for copy in copies:
            copy.start()
            pending.append(copy)

    def z_stage(j):
        for kk in range(2):
            rows = pl.ds(aligned((w_of(j) * 4 + y) * 2 + kk, 32), 32)
            pltpu.make_async_copy(g_ref.at[rows, q_lanes], g_ref.at[rows, q_lanes], tr.at[w_of(j) * 2 + kk]).wait()
        send(z_copies(j))

    def y_stage(j):
        for copy in z_copies(j):
            copy.wait_recv()
        send(y_copies(j))

    def product_stage(j):
        for copy in y_copies(j):
            copy.wait_recv()
        rows = pl.ds(aligned(w_of(j), 256), 256)

        def tile(t, _):
            cols = pl.ds(aligned(t, 256), 256)
            part = lax.dot_general(g_ref[rows, :], a_ref[cols, :], (((1,), (1,)), ((), ())),
                                   preferred_element_type=F32)
            p_ref[:, cols] = part
            return 0

        lax.fori_loop(0, 4, tile, 0)
        for s in range(4):
            cs_ref[j, s * 32:(s + 1) * 32, :] = p_ref[pl.ds(aligned(s * 2 + 1 - k, 32), 32), :].astype(BF16)
        send([core_copy(j)])

    def x_stage(j):
        core_copy(j).wait_recv()
        for o in range(4):
            s = (x + o) % 4
            both = (p_ref[pl.ds(aligned(s * 2 + k, 32), 32), :]
                    + cr_ref[j, pl.ds(aligned(s, 32), 32), :].astype(F32))
            if o:
                xs_ref[j, o - 1] = both.astype(BF16)
            else:
                xo_ref[j] = both
        send(x_copies(j))

    def h_stage(j):
        for copy in x_copies(j):
            copy.wait_recv()
        total = xo_ref[j]
        for o in range(3):
            total += xr_ref[j, o].astype(F32)
        if OFFS[j]:
            zs_ref[OFFS[j] - 1] = total.astype(BF16)
            send([h_copy(OFFS[j])])
        else:
            xo_ref[j] = total

    a_copy.wait()
    for j in range(4):
        z_stage(j)
    for j in range(4):
        y_stage(j)
    product_stage(0)
    x_stage(0)
    for j in range(1, 4):
        product_stage(j)
        x_stage(j)
        h_stage(j - 1)
    h_stage(3)
    total = xo_ref[OFFS.index(0)]
    for o in range(1, 4):
        h_copy(o).wait_recv()
        total += zr_ref[o - 1].astype(F32)
    share = jnp.sum(ft_ref[...].astype(F32) * total, axis=1, keepdims=True)
    wide = jnp.concatenate([jnp.broadcast_to(share, (32, 128)), jnp.zeros((96, 128), F32)], axis=0)
    dz_ref[0] = wide.T[:8]
    copies = [pltpu.make_async_remote_copy(
        dz_ref.at[0], dz_ref.at[o], ds_.at[o - 1], dr.at[o - 1],
        device_id=(row_of((zl + o) % 8, y), c), device_id_type=MESH) for o in range(1, 8)]
    send(copies)
    out_ref[...] = (-(mask_ref[...] * total)).astype(BF16)
    for copy in copies:
        copy.wait_recv()
    line = dz_ref[0]
    for o in range(1, 8):
        line += dz_ref[o]
    dy_ref[0] = line
    copies = [pltpu.make_async_remote_copy(
        dy_ref.at[0], dy_ref.at[o], es.at[o - 1], er.at[o - 1],
        device_id=(row_of(zl, (y + o) % 4), c), device_id_type=MESH) for o in range(1, 4)]
    send(copies)
    for copy in copies:
        copy.wait_recv()
    for o in range(1, 4):
        line += dy_ref[o]
    diag_ref[...] = base_ref[...] + line[0:1, 0:32]

    for here, remote in t_copies:
        pl.when(jnp.logical_not(here))(remote.wait_send)
    for copy in pending:
        copy.wait_send()


def body(factor_panel, ancestor_inverse, pattern, diag_base):
    vmem = pl.BlockSpec(memory_space=pltpu.VMEM)
    dma = pltpu.SemaphoreType.DMA
    out, diag = pl.pallas_call(
        kernel,
        out_shape=(jax.ShapeDtypeStruct((32, 1024), BF16), jax.ShapeDtypeStruct((1, 32), F32)),
        in_specs=[pl.BlockSpec(memory_space=pltpu.SMEM), vmem, vmem, pl.BlockSpec(memory_space=pl.ANY)],
        out_specs=(vmem, vmem),
        scratch_shapes=[
            pltpu.VMEM((1024, 1024), BF16),
            pltpu.VMEM((32, 1024), F32),
            pltpu.VMEM((32, 1024), BF16),
            pltpu.VMEM((1024, 1024), BF16),
            pltpu.VMEM((256, 1024), F32),
            pltpu.VMEM((4, 128, 1024), BF16),
            pltpu.VMEM((4, 128, 1024), BF16),
            pltpu.VMEM((4, 3, 32, 1024), BF16),
            pltpu.VMEM((4, 3, 32, 1024), BF16),
            pltpu.VMEM((4, 32, 1024), F32),
            pltpu.VMEM((3, 32, 1024), BF16),
            pltpu.VMEM((3, 32, 1024), BF16),
            pltpu.VMEM((8, 8, 128), F32),
            pltpu.VMEM((4, 8, 128), F32),
            dma, dma((8,)), dma((8,)), dma((12,)), dma((12,)), dma((12,)), dma((12,)),
            dma((4,)), dma((4,)), dma((12,)), dma((12,)), dma((3,)), dma((3,)),
            dma((7,)), dma((7,)), dma((3,)), dma((3,)),
        ],
        compiler_params=pltpu.CompilerParams(collective_id=0, has_side_effects=True, vmem_limit_bytes=60 << 20),
        name="selected_inverse",
    )(pattern, factor_panel.T, diag_base.reshape(1, 32), ancestor_inverse)
    return out.T, diag.reshape(32)


def solution(mesh):
    placed = (P("row", "col"), P("row", "col"), P(), P("col"))
    return jax.shard_map(
        body, mesh=mesh, in_specs=placed, out_specs=(P("row", "col"), P("col")), check_vma=False
    )
```

time: 987 us -> 119 us (0.12)
  the two profiles are of different devices: /device:TPU:4 before, /device:TPU:8 now
where the time goes in v1:
time: 119 us
  Pallas kernels  116 us (97%)
  local copies, waits for them, and re-layouts  2.59 us (2%)
    pallas_call x1, Pallas kernels, body(): pl.pallas_call(kernel, out_shape=(jax.ShapeDtypeStruct((32, 1024), BF16),...  116 us
    unnamed x2, local copies, waits for them, and re-layouts  2.59 us

profile of v1, /device:TPU:8, one launch (start us, length us, event | category | flops | bytes accessed | tf_op | source)
XLA Modules:
  0.0 118.9 jit_solution(16137510658458982353)
XLA Ops:
  0.6 115.7 %selected_inverse.1 = (bf16[32,1024]{1,0:T(8,128)(2,1)}, f32[1,32]{1,0:T(1,128)}) custom-call(s32[256]{0:T(256)} %pattern_ref.1, bf16[32,1024]{1,0:T(8,128)(2,1)} %bitcast.4, f32[1,32]{1,0:T(1,128)} %bitcast.6, bf16[1024,1024]{1,0:T(8,128)(2,1)} %a_hbm.1), custom_call_target="tpu_custom_call" | custom-call | tf_op jit(solution)/shard_map/selected_inverse/pallas_call | solution.py:216
  116.3 1.5 %copy.8 = bf16[1024,32]{0,1:T(8,128)(2,1)} copy(bf16[1024,32]{0,1:T(8,128)(2,1)} %bitcast.5) | data formatting | bytes 131072
  117.8 1.1 copy.9

commit v2 on v1

v2 whole, which is shorter than its diff:
```python
import jax
import jax.numpy as jnp
from jax import lax
from jax.experimental import pallas as pl
from jax.experimental.pallas import tpu as pltpu
from jax.sharding import PartitionSpec as P

MESH = pl.DeviceIdType.MESH
BF16 = jnp.bfloat16
F32 = jnp.float32
ORDER = ((0, 0), (0, 1), (0, 3), (0, 2), (1, 0), (1, 1), (1, 3), (1, 2))
LANDING = (0, 1, 3, 2)
AHEAD = 3


def aligned(i, n):
    return pl.multiple_of(i * n, n)


def kernel(pattern_ref, f_ref, base_ref, a_hbm, out_ref, diag_ref,
           a_ref, mask_ref, ft_ref, g_ref, p_ref, cs_ref, cr_ref, xs_ref, xr_ref, xo_ref,
           own_ref, zs_ref, zr_ref, dz_ref, dy_ref,
           a_sem, ts, tr, zs, zr, ys, yr, cs, cr, xs, xr, hs, hr, ds_, dr, es, er):
    r, c = lax.axis_index("row"), lax.axis_index("col")
    zl, y = r // 4, r % 4
    zh, x, k = c // 8, (c // 2) % 4, c % 2
    half, q = zl // 4, zl % 4

    def row_of(zl_, y_):
        return zl_ * 4 + y_

    def col_of(zh_, x_, k_):
        return (zh_ * 4 + x_) * 2 + k_

    barrier = pltpu.get_barrier_semaphore()

    def greet(dev):
        pl.semaphore_signal(barrier, inc=1, device_id=dev, device_id_type=MESH)

    a_copy = pltpu.make_async_copy(a_hbm, a_ref, a_sem)
    a_copy.start()
    for i in range(8):
        src_col = (i // 2 * 4 + y) * 2 + i % 2
        pl.when(jnp.logical_or(c != r, src_col != c))(lambda s=src_col: greet((c, s)))
    for o in range(1, 4):
        greet((r, col_of((zh + o) % 4, x, k)))
    for o in range(1, 8):
        greet((row_of((zl + o) % 8, y), c))
    for o in range(1, 4):
        greet((row_of(zl, (y + o) % 4), c))
        greet((r, col_of(zh, (x + o) % 4, k)))
    greet((r, col_of(zh, x, 1 - k)))

    for b in range(8):
        m = pattern_ref[r * 8 + b].astype(F32)
        mask_ref[:, b * 128:(b + 1) * 128] = jnp.full((32, 128), m, F32)
    ft_ref[...] = (f_ref[...].astype(F32) * mask_ref[...]).astype(BF16)

    self_t = jnp.logical_and(c == r, row_of(zl, x) == r)
    pl.semaphore_wait(barrier, 25 - self_t.astype(jnp.int32))

    pending = []
    q_lanes = pl.ds(aligned(q, 256), 256)
    t_rows = pl.ds(aligned(x * 2 + k, 16), 16)
    own_rows = pl.ds(aligned(y, 32), 32)

    def t_copies(b):
        src = pl.ds(b * 16, 16)
        sem = (b * 4 + zh) * 2 + k
        for h in range(2):
            for p in range(4):
                lanes = pl.ds(p * 256, 256)
                there = row_of(h * 4 + p, x)
                here = jnp.logical_and(c == r, there == r)
                remote = pltpu.make_async_remote_copy(
                    ft_ref.at[src, lanes], g_ref.at[b, zh, t_rows, lanes], ts.at[b * 8 + h * 4 + p], tr.at[sem],
                    device_id=(there, r), device_id_type=MESH)
                local = pltpu.make_async_copy(
                    ft_ref.at[src, lanes], g_ref.at[b, zh, t_rows, lanes], tr.at[sem])
                yield here, remote, local

    def t_start(b):
        for here, remote, local in t_copies(b):
            pl.when(jnp.logical_not(here))(remote.start)
            pl.when(here)(local.start)

    def t_sent(b):
        for here, remote, _ in t_copies(b):
            pl.when(jnp.logical_not(here))(remote.wait_send)

    def z_copies(b, w):
        part = g_ref.at[b, w, own_rows, q_lanes]
        at = b * 12 + w * 3 - 1
        return [pltpu.make_async_remote_copy(
            part, part, zs.at[at + d], zr.at[at + d],
            device_id=(row_of(half * 4 + (q + d) % 4, y), c), device_id_type=MESH) for d in range(1, 4)]

    def y_copies(b, w):
        part = g_ref.at[b, w, own_rows, :]
        at = b * 12 + w * 3 - 1
        return [pltpu.make_async_remote_copy(
            part, part, ys.at[at + d], yr.at[at + d],
            device_id=(row_of(zl, (y + d) % 4), c), device_id_type=MESH) for d in range(1, 4)]

    def core_copy(n):
        return pltpu.make_async_remote_copy(
            cs_ref.at[n], cr_ref.at[n], cs.at[n], cr.at[n],
            device_id=(r, col_of(zh, x, 1 - k)), device_id_type=MESH)

    def x_copies(n):
        return [pltpu.make_async_remote_copy(
            xs_ref.at[n, d - 1], xr_ref.at[n, d - 1], xs.at[n * 3 + d - 1], xr.at[n * 3 + d - 1],
            device_id=(r, col_of(zh, (x + d) % 4, k)), device_id_type=MESH) for d in range(1, 4)]

    def h_copy(b, w):
        return pltpu.make_async_remote_copy(
            zs_ref.at[b, w], zr_ref.at[b, zh], hs.at[b * 4 + w], hr.at[b * 4 + zh],
            device_id=(r, col_of(w, x, k)), device_id_type=MESH)

    def h_landed(b, w):
        return pltpu.make_async_copy(zr_ref.at[b, w], zr_ref.at[b, w], hr.at[b * 4 + w])

    def send(copies):
        for copy in copies:
            copy.start()
            pending.append(copy)

    def z_stage(b, w):
        for kk in range(2):
            part = g_ref.at[b, w, pl.ds(aligned(y * 2 + kk, 16), 16), q_lanes]
            pltpu.make_async_copy(part, part, tr.at[(b * 4 + w) * 2 + kk]).wait()
        send(z_copies(b, w))

    def y_stage(n):
        b, w = ORDER[n]
        for copy in z_copies(b, w):
            copy.wait_recv()
        send(y_copies(b, w))

    def product_stage(n):
        b, w = ORDER[n]
        for copy in y_copies(b, w):
            copy.wait_recv()
        if n + AHEAD < 8:
            y_stage(n + AHEAD)

        def tile(t, _):
            cols = pl.ds(aligned(t, 256), 256)
            p_ref[n % 2, :, cols] = lax.dot_general(
                g_ref[b, w], a_ref[cols, :], (((1,), (1,)), ((), ())), preferred_element_type=F32)
            return 0

        lax.fori_loop(0, 4, tile, 0)
        for s in range(4):
            cs_ref[n, s * 16:(s + 1) * 16, :] = p_ref[n % 2, pl.ds(aligned(s * 2 + 1 - k, 16), 16), :].astype(BF16)
        send([core_copy(n)])

    def x_stage(n):
        core_copy(n).wait_recv()
        for d in range(4):
            s = (x + d) % 4
            both = (p_ref[n % 2, pl.ds(aligned(s * 2 + k, 16), 16), :]
                    + cr_ref[n, pl.ds(aligned(s, 16), 16), :].astype(F32))
            if d:
                xs_ref[n, d - 1] = both.astype(BF16)
            else:
                xo_ref[n] = both
        send(x_copies(n))

    def h_stage(n):
        b, w = ORDER[n]
        for copy in x_copies(n):
            copy.wait_recv()
        total = xo_ref[n]
        for d in range(3):
            total += xr_ref[n, d].astype(F32)

        @pl.when(zh == w)
        def _():
            own_ref[b] = total

        @pl.when(zh != w)
        def _():
            zs_ref[b, w] = total.astype(BF16)
            h_copy(b, w).start()

    for b in range(2):
        t_start(b)
    for w in LANDING:
        z_stage(0, w)
    a_copy.wait()
    for n in range(AHEAD):
        y_stage(n)
    for w in LANDING:
        z_stage(1, w)
    for n in range(10):
        if n < 8:
            product_stage(n)
        if 1 <= n < 9:
            x_stage(n - 1)
        if n >= 2:
            h_stage(n - 2)

    totals = []
    for b in range(2):
        zr_ref[b, zh] = jnp.zeros((16, 1024), BF16)
        for w in range(4):
            pl.when(zh != w)(h_landed(b, w).wait)
        total = own_ref[b]
        for w in range(4):
            total += zr_ref[b, w].astype(F32)
        totals.append(total)
    total = jnp.concatenate(totals, axis=0)
    share = jnp.sum(ft_ref[...].astype(F32) * total, axis=1, keepdims=True)
    wide = jnp.concatenate([jnp.broadcast_to(share, (32, 128)), jnp.zeros((96, 128), F32)], axis=0)
    dz_ref[0] = wide.T[:1]
    copies = [pltpu.make_async_remote_copy(
        dz_ref.at[0], dz_ref.at[o], ds_.at[o - 1], dr.at[o - 1],
        device_id=(row_of((zl + o) % 8, y), c), device_id_type=MESH) for o in range(1, 8)]
    send(copies)
    out_ref[...] = (-(mask_ref[...] * total)).astype(BF16)
    for copy in copies:
        copy.wait_recv()
    line = dz_ref[0]
    for o in range(1, 8):
        line += dz_ref[o]
    dy_ref[0] = line
    copies = [pltpu.make_async_remote_copy(
        dy_ref.at[0], dy_ref.at[o], es.at[o - 1], er.at[o - 1],
        device_id=(row_of(zl, (y + o) % 4), c), device_id_type=MESH) for o in range(1, 4)]
    send(copies)
    for copy in copies:
        copy.wait_recv()
    for o in range(1, 4):
        line += dy_ref[o]
    diag_ref[...] = base_ref[...] + line[:, 0:32]

    for b in range(2):
        t_sent(b)
        for w in range(4):
            pl.when(zh != w)(h_copy(b, w).wait_send)
    for copy in pending:
        copy.wait_send()


def body(factor_panel, ancestor_inverse, pattern, diag_base):
    vmem = pl.BlockSpec(memory_space=pltpu.VMEM)
    dma = pltpu.SemaphoreType.DMA
    out, diag = pl.pallas_call(
        kernel,
        out_shape=(jax.ShapeDtypeStruct((32, 1024), BF16), jax.ShapeDtypeStruct((1, 32), F32)),
        in_specs=[pl.BlockSpec(memory_space=pltpu.SMEM), vmem, vmem, pl.BlockSpec(memory_space=pl.ANY)],
        out_specs=(vmem, vmem),
        scratch_shapes=[
            pltpu.VMEM((1024, 1024), BF16),
            pltpu.VMEM((32, 1024), F32),
            pltpu.VMEM((32, 1024), BF16),
            pltpu.VMEM((2, 4, 128, 1024), BF16),
            pltpu.VMEM((2, 128, 1024), F32),
            pltpu.VMEM((8, 64, 1024), BF16),
            pltpu.VMEM((8, 64, 1024), BF16),
            pltpu.VMEM((8, 3, 16, 1024), BF16),
            pltpu.VMEM((8, 3, 16, 1024), BF16),
            pltpu.VMEM((8, 16, 1024), F32),
            pltpu.VMEM((2, 16, 1024), F32),
            pltpu.VMEM((2, 4, 16, 1024), BF16),
            pltpu.VMEM((2, 4, 16, 1024), BF16),
            pltpu.VMEM((8, 1, 128), F32),
            pltpu.VMEM((4, 1, 128), F32),
            dma, dma((16,)), dma((16,)), dma((24,)), dma((24,)), dma((24,)), dma((24,)),
            dma((8,)), dma((8,)), dma((24,)), dma((24,)), dma((8,)), dma((8,)),
            dma((7,)), dma((7,)), dma((3,)), dma((3,)),
        ],
        compiler_params=pltpu.CompilerParams(collective_id=0, has_side_effects=True, vmem_limit_bytes=60 << 20),
        name="selected_inverse",
    )(pattern, factor_panel.T, diag_base.reshape(1, 32), ancestor_inverse)
    return out.T, diag.reshape(32)


def solution(mesh):
    placed = (P("row", "col"), P("row", "col"), P(), P("col"))
    return jax.shard_map(
        body, mesh=mesh, in_specs=placed, out_specs=(P("row", "col"), P("col")), check_vma=False
    )
```

time: 119 us -> 111 us (0.933)
  the two profiles are of different devices: /device:TPU:8 before, /device:TPU:34 now
where the time goes in v2:
time: 111 us; the launch traced here: 110 us
  Pallas kernels  107 us (96%)
  local copies, waits for them, and re-layouts  2.59 us (2%)
    pallas_call x1, Pallas kernels, body(): pl.pallas_call(kernel, out_shape=(jax.ShapeDtypeStruct((32, 1024), BF16),...  107 us
    unnamed x2, local copies, waits for them, and re-layouts  2.59 us

profile of v2, /device:TPU:34, one launch (start us, length us, event | category | flops | bytes accessed | tf_op | source)
XLA Modules:
  0.0 110.4 jit_solution(13724985535184701036)
XLA Ops:
  0.6 107.2 %selected_inverse.1 = (bf16[32,1024]{1,0:T(8,128)(2,1)}, f32[1,32]{1,0:T(1,128)}) custom-call(s32[256]{0:T(256)} %pattern_ref.1, bf16[32,1024]{1,0:T(8,128)(2,1)} %bitcast.4, f32[1,32]{1,0:T(1,128)} %bitcast.6, bf16[1024,1024]{1,0:T(8,128)(2,1)} %a_hbm.1), custom_call_target="tpu_custom_call" | custom-call | tf_op jit(solution)/shard_map/selected_inverse/pallas_call | solution.py:249
  107.8 1.5 %copy.8 = bf16[1024,32]{0,1:T(8,128)(2,1)} copy(bf16[1024,32]{0,1:T(8,128)(2,1)} %bitcast.5) | data formatting | bytes 131072
  109.3 1.1 %copy.9 = f32[32]{0:T(128)} copy(f32[32]{0:T(128)} %bitcast.7) | data formatting | bytes 256

commit v3 on v2

--- a/solution.py
+++ b/solution.py
@@ -19,8 +19,8 @@
 
 def kernel(pattern_ref, f_ref, base_ref, a_hbm, out_ref, diag_ref,
            a_ref, mask_ref, ft_ref, g_ref, p_ref, cs_ref, cr_ref, xs_ref, xr_ref, xo_ref,
-           own_ref, zs_ref, zr_ref, dz_ref, dy_ref,
-           a_sem, ts, tr, zs, zr, ys, yr, cs, cr, xs, xr, hs, hr, ds_, dr, es, er):
+           own_ref, zs_ref, zr_ref, dz_ref,
+           a_sem, ts, tr, zs, zr, ys, yr, cs, cr, xs, xr, hs, hr, ds_, dr):
     r, c = lax.axis_index("row"), lax.axis_index("col")
     zl, y = r // 4, r % 4
     zh, x, k = c // 8, (c // 2) % 4, c % 2
@@ -44,12 +44,17 @@
         pl.when(jnp.logical_or(c != r, src_col != c))(lambda s=src_col: greet((c, s)))
     for o in range(1, 4):
         greet((r, col_of((zh + o) % 4, x, k)))
-    for o in range(1, 8):
-        greet((row_of((zl + o) % 8, y), c))
     for o in range(1, 4):
-        greet((row_of(zl, (y + o) % 4), c))
         greet((r, col_of(zh, (x + o) % 4, k)))
     greet((r, col_of(zh, x, 1 - k)))
+
+    def each_row_peer(act):
+        def step(o, _):
+            act((r + o) % 32)
+            return 0
+        lax.fori_loop(1, 32, step, 0)
+
+    each_row_peer(lambda peer: greet((peer, c)))
 
     for b in range(8):
         m = pattern_ref[r * 8 + b].astype(F32)
@@ -57,7 +62,7 @@
     ft_ref[...] = (f_ref[...].astype(F32) * mask_ref[...]).astype(BF16)
 
     self_t = jnp.logical_and(c == r, row_of(zl, x) == r)
-    pl.semaphore_wait(barrier, 25 - self_t.astype(jnp.int32))
+    pl.semaphore_wait(barrier, 46 - self_t.astype(jnp.int32))
 
     pending = []
     q_lanes = pl.ds(aligned(q, 256), 256)
@@ -213,28 +218,21 @@
     total = jnp.concatenate(totals, axis=0)
     share = jnp.sum(ft_ref[...].astype(F32) * total, axis=1, keepdims=True)
     wide = jnp.concatenate([jnp.broadcast_to(share, (32, 128)), jnp.zeros((96, 128), F32)], axis=0)
-    dz_ref[0] = wide.T[:1]
-    copies = [pltpu.make_async_remote_copy(
-        dz_ref.at[0], dz_ref.at[o], ds_.at[o - 1], dr.at[o - 1],
-        device_id=(row_of((zl + o) % 8, y), c), device_id_type=MESH) for o in range(1, 8)]
-    send(copies)
+    dz_ref[r] = wide.T[:1]
+
+    def share_copy(peer):
+        return pltpu.make_async_remote_copy(
+            dz_ref.at[r], dz_ref.at[r], ds_.at[peer], dr.at[r], device_id=(peer, c), device_id_type=MESH)
+
+    def share_landed(peer):
+        return pltpu.make_async_copy(dz_ref.at[peer], dz_ref.at[peer], dr.at[peer])
+
+    each_row_peer(lambda peer: share_copy(peer).start())
     out_ref[...] = (-(mask_ref[...] * total)).astype(BF16)
-    for copy in copies:
-        copy.wait_recv()
-    line = dz_ref[0]
-    for o in range(1, 8):
-        line += dz_ref[o]
-    dy_ref[0] = line
-    copies = [pltpu.make_async_remote_copy(
-        dy_ref.at[0], dy_ref.at[o], es.at[o - 1], er.at[o - 1],
-        device_id=(row_of(zl, (y + o) % 4), c), device_id_type=MESH) for o in range(1, 4)]
-    send(copies)
-    for copy in copies:
-        copy.wait_recv()
-    for o in range(1, 4):
-        line += dy_ref[o]
-    diag_ref[...] = base_ref[...] + line[:, 0:32]
-
+    each_row_peer(lambda peer: share_landed(peer).wait())
+    diag_ref[...] = base_ref[...] + jnp.sum(dz_ref[...], axis=0)[:, 0:32]
+
+    each_row_peer(lambda peer: share_copy(peer).wait_send())
     for b in range(2):
         t_sent(b)
         for w in range(4):
@@ -265,11 +263,10 @@
             pltpu.VMEM((2, 16, 1024), F32),
             pltpu.VMEM((2, 4, 16, 1024), BF16),
             pltpu.VMEM((2, 4, 16, 1024), BF16),
-            pltpu.VMEM((8, 1, 128), F32),
-            pltpu.VMEM((4, 1, 128), F32),
+            pltpu.VMEM((32, 1, 128), F32),
             dma, dma((16,)), dma((16,)), dma((24,)), dma((24,)), dma((24,)), dma((24,)),
             dma((8,)), dma((8,)), dma((24,)), dma((24,)), dma((8,)), dma((8,)),
-            dma((7,)), dma((7,)), dma((3,)), dma((3,)),
+            dma((32,)), dma((32,)),
         ],
         compiler_params=pltpu.CompilerParams(collective_id=0, has_side_effects=True, vmem_limit_bytes=60 << 20),
         name="selected_inverse",

time: 111 us -> 111 us (level)
  the two profiles are of different devices: /device:TPU:34 before, /device:TPU:4 now
where the time goes in v3:
time: 111 us; the launch traced here: 110 us
  Pallas kernels  107 us (96%)
  local copies, waits for them, and re-layouts  2.59 us (2%)
    pallas_call x1, Pallas kernels, body(): pl.pallas_call(kernel, out_shape=(jax.ShapeDtypeStruct((32, 1024), BF16),...  107 us
    unnamed x2, local copies, waits for them, and re-layouts  2.59 us

profile of v3, /device:TPU:4, one launch (start us, length us, event | category | flops | bytes accessed | tf_op | source)
XLA Modules:
  0.0 110.5 jit_solution(10213411132885047481)
XLA Ops:
  0.6 107.3 %selected_inverse.1 = (bf16[32,1024]{1,0:T(8,128)(2,1)}, f32[1,32]{1,0:T(1,128)}) custom-call(s32[256]{0:T(256)} %pattern_ref.1, bf16[32,1024]{1,0:T(8,128)(2,1)} %bitcast.4, f32[1,32]{1,0:T(1,128)} %bitcast.6, bf16[1024,1024]{1,0:T(8,128)(2,1)} %a_hbm.1), custom_call_target="tpu_custom_call" | custom-call | tf_op jit(solution)/shard_map/selected_inverse/pallas_call | solution.py:247
  107.9 1.5 %copy.8 = bf16[1024,32]{0,1:T(8,128)(2,1)} copy(bf16[1024,32]{0,1:T(8,128)(2,1)} %bitcast.5) | data formatting | bytes 131072
  109.4 1.1 %copy.9 = f32[32]{0:T(128)} copy(f32[32]{0:T(128)} %bitcast.7) | data formatting | bytes 256
